TPU v7x, 512 devices: a whole 4x8x8 slice. The times are simulated.
512 devices in a mesh: tm: 16 (over x, z_hi, core), cell: 32 (over y, z_lo).
Axes of the slice: x: 4, y: 8, z: 8 (z_hi: 2, z_lo: 4; z = z_hi * 4 + z_lo), core: 2. Of those that a mesh axis runs over, the one named last changes fastest.
Arguments:
- sensitivity: bfloat16 [2048, 16, 16384], P(None, 'tm', 'cell'), may hold values from -0.25 to 0.25
- duals: bfloat16 [2048, 128], P(('tm', 'cell')), may hold values from -6 to 6
- time_cov: float32 [16, 16], replicated, may hold values from 0.05 to 0.5
- cell_coords: int32 [2, 16384], P(None, 'cell'), may hold values from 0 to 127, as said below
- obs_time: int32 [2048], replicated, may hold values from 0 to 15
- obs_owner: int32 [2048], replicated, may hold values from 0 to 2047, each once
Outputs:
- product: float32 [2048, 128], P(('tm', 'cell'))
Inputs may be any that keep to these rules, and one draw needn't show every extreme that they name: `cell_coords`: every cell has its own grid position; rows lie below 128 and columns below 128. `obs_owner`: every observation stands in exactly one slot.
All inputs are finite; a program needn't handle non-finite values.
Results may differ from a plain program's by a relative error of at most 0.0049.
Values may be sent and summed in bfloat16 or wider, within the bound.
No kernel may reach another device: no remote copies, remote signals or barrier semaphores. Data moves between devices by JAX's collectives and lax.ppermute only.
A program may use at most 64 MiB of HBM per device.

v0:
```python
import jax
import jax.numpy as jnp
from jax import lax
from jax.sharding import Mesh
from jax.sharding import PartitionSpec as P

LSCALE = 4
TM = ("tm_0", "tm_1", "tm_2")
TM_CELL = ("tm_0", "tm_1", "tm_2", "cell_0", "cell_1")
CELL = ("cell_0", "cell_1")


def laid_out(pieces, dim):
    pieces = jnp.moveaxis(pieces, 0, dim)
    shape = pieces.shape
    return pieces.reshape(*shape[:dim], shape[dim] * shape[dim + 1], *shape[dim + 2 :])


def sent_to_all(array, axis):
    copies = jnp.broadcast_to(array, (lax.axis_size(axis), *array.shape))
    return lax.all_to_all(copies, axis, split_axis=0, concat_axis=0, tiled=True)


def gathered_copies(array, axis, dim):
    return laid_out(sent_to_all(array, axis), dim)


def cut_along(array, dim, length):
    shape = array.shape
    pieces = array.reshape(*shape[:dim], length, shape[dim] // length, *shape[dim + 1 :])
    return jnp.moveaxis(pieces, dim, 0)


def edges_of(length, count):
    hop = length // count
    if hop >= 8:
        hop -= hop % 8
    return [hop * k for k in range(1, count)]


def own_block(pieces, axes, sequence):
    inside = pieces.shape[1:]
    pieces = pieces.reshape(*(lax.axis_size(a) for a in axes), *inside)
    pieces = jnp.moveaxis(pieces, sequence, range(len(axes))).reshape(-1, *inside)
    for k in sequence:
        pieces = lax.psum_scatter(pieces, axes[k], scatter_dimension=0, tiled=True)
    return pieces[0]


def sum_at_once(array, axes, dim):
    pieces = cut_along(array, dim, lax.axis_size(axes))
    widest = max(range(1, max(2, pieces.ndim - 1)), key=lambda d: pieces.shape[d])
    count, done = (len(axes), [])
    for first, slab in enumerate(
        jnp.split(pieces, edges_of(pieces.shape[widest], count), axis=widest)
    ):
        if slab.size:
            sequence = [(first + k) % count for k in range(count)]
            done.append(own_block(slab, axes, sequence))
    return jnp.concatenate(done, axis=widest - 1)


def covariance(left_coords, right_coords):
    row_gap = (left_coords[0][:, None] - right_coords[0][None, :]).astype(jnp.float32)
    col_gap = (left_coords[1][:, None] - right_coords[1][None, :]).astype(jnp.float32)
    distance = jnp.sqrt(row_gap * row_gap + col_gap * col_gap)
    return (jnp.exp(-distance / LSCALE) / (8.0 * LSCALE)).astype(jnp.bfloat16)


def per_device(sensitivity, duals, time_cov, cell_coords, obs_time, obs_owner):
    obs_count = sensitivity.shape[0]
    time_count = sensitivity.shape[1]
    cell_count = sensitivity.shape[2]
    real_count = duals.shape[1]
    first_time = lax.axis_index(TM) * time_count
    time_index = first_time + jnp.arange(time_count, dtype=jnp.int32)
    live = time_index[None, :, None] <= obs_time[:, None, None]
    masked = jnp.where(live, sensitivity, jnp.zeros((), jnp.bfloat16))
    flattened = masked.reshape(obs_count, time_count * cell_count)
    picked = flattened
    adjoint = lax.dot_general(
        picked,
        lax.all_gather(duals, TM_CELL, axis=0, tiled=True),
        (((0,), (0,)), ((), ())),
        preferred_element_type=jnp.float32,
    )
    local_adj = (
        adjoint.astype(jnp.bfloat16).reshape(time_count, cell_count, real_count).transpose(1, 0, 2)
    )
    all_coords = gathered_copies(cell_coords, CELL, 1)
    spread_adj = lax.all_to_all(local_adj, TM, split_axis=2, concat_axis=1, tiled=True)
    values = jnp.einsum(
        "st,ctr->csr", time_cov, spread_adj.astype(jnp.float32), precision=lax.Precision.HIGHEST
    ).astype(jnp.bfloat16)
    portion = lax.all_gather(values, CELL, axis=0, tiled=True)
    kernel = covariance(cell_coords, all_coords)
    summed = jnp.dot(
        kernel, portion.reshape(portion.shape[0], -1), preferred_element_type=jnp.float32
    )
    weighted = lax.all_to_all(
        summed.reshape(values.shape).astype(jnp.bfloat16),
        TM,
        split_axis=1,
        concat_axis=2,
        tiled=True,
    )
    weighted_flat = weighted.transpose(1, 0, 2).reshape(time_count * cell_count, real_count)
    picked = jnp.take(flattened, obs_owner, axis=0)
    return sum_at_once(
        jnp.dot(picked, weighted_flat, preferred_element_type=jnp.float32), TM_CELL, 0
    )


def solution(mesh):
    split = Mesh(mesh.devices.reshape(4, 2, 2, 8, 4), ("tm_0", "tm_1", "tm_2", "cell_0", "cell_1"))
    return jax.shard_map(
        per_device,
        mesh=split,
        in_specs=(P(None, TM, CELL), P(TM_CELL, None), P(), P(None, CELL), P(), P()),
        out_specs=P(TM_CELL, None),
        check_vma=False,
    )
```

profile of v0, /device:TPU:2, one launch (start us, length us, event | category | flops | bytes accessed | tf_op | source)
XLA Modules:
  0.0 1611.9 jit_solution(16433688849147574105)
XLA Ops:
  6.5 1138.5 %all-gather = bf16[512,4,128]{2,1,0:T(4,128)(2,1)S(1)} all-gather(bf16[1,4,128]{2,1,0:T(4,128)(2,1)} %bitcast.57), channel_id=1, replica_groups=mesh['tm_0'=4,'tm_1'=2,'tm_2'=2,'cell_0'=8,'cell_1'=4] {'tm_0','tm_1','t..., dimensions={0}, use_global_device_ids=true | all-gather | bytes 525312 | tf_op jit(solution)/shard_map/all_gather | solution.py:83
  1145.7 1.8 select_bitcast_fusion
  1147.5 0.8 fusion.14
  1149.0 1.4 reduce
  1150.5 126.0 %all_to_all.26 = bf16[16,2,2048]{2,1,0:T(2,128)(2,1)S(1)} all-to-all(bf16[16,2,2048]{2,1,0:T(2,128)(2,1)S(1)} %reshape.87), channel_id=1, replica_groups=mesh['tm_0'=4,'tm_1'=2,'tm_2'=2,'cell_0'=8,'cell_1'=4] {'tm_0','tm_1','t..., dimensions={0} | all-to-all | bytes 262144 | tf_op jit(solution)/shard_map/all_to_all | solution.py:91
  1276.7 0.9 fusion.15
  1278.3 3.9 all-to-all-start
  1282.2 9.2 gather_fusion
  1291.4 3.9 all-to-all-done
  1295.4 136.2 %all-gather.3.cloned.1.call-done = bf16[16384,16,8]{0,1,2:T(8,128)(2,1)} async-done(((bf16[512,16,8]{0,1,2:T(8,128)(2,1)}), bf16[16384,16,8]{0,1,2:T(8,128)(2,1)}) %all-gather.3.cloned.1.call-update) | async-done | bytes 4194320 | tf_op jit(solution)/shard_map/all_gather | solution.py:95
  1431.6 22.9 %fusion.9 = bf16[512,16,8]{0,1,2:T(8,128)(2,1)S(1)} fusion(bf16[16384,16,8]{0,1,2:T(8,128)(2,1)} %all-gather.3.cloned.1.call-done, s32[16384]{0:T(1024)S(1)} %bitcast.54, s32[512]{0:T(512)S(1)} %bitcast.56, s32[16384]{0:T(1024)S(1)} %bitcast.53, s32[512]{0:T(512)S(1)} %bitcast.55), kind=kOutput, calls=%fused_computation.12 | convolution fusion | flops 2239823872 | bytes 4460544 | tf_op jit(solution)/shard_map/dot_general | solution.py:97
  1455.3 7.0 all-to-all-start.2
  1462.3 1.6 broadcast_select_fusion
  1463.9 2.5 select_n.30
  1466.4 4.6 all-to-all-done.2
  1471.0 1.3 fusion.6
  1472.3 1.1 copy.24
  1473.5 32.9 %reduce-scatter.5.cloned.1.call-done = f32[128,4,128]{2,0,1:T(8,128)} async-done(((f32[512,4,128]{2,0,1:T(8,128)}), f32[128,4,128]{2,0,1:T(8,128)}) %reduce-scatter.5.cloned.1.call-update) | async-done | bytes 262160 | tf_op jit(solution)/shard_map/reduce_scatter | solution.py:46
  1506.5 26.7 %reduce-scatter.7.cloned.1.call-done = f32[32,4,128]{2,0,1:T(8,128)} async-done(((f32[128,4,128]{2,0,1:T(8,128)}), f32[32,4,128]{2,0,1:T(8,128)}) %reduce-scatter.7.cloned.1.call-update) | async-done | bytes 65552 | tf_op jit(solution)/shard_map/reduce_scatter | solution.py:46
  1533.2 26.2 %reduce-scatter.9.cloned.1.call-done = f32[16,4,128]{2,0,1:T(8,128)} async-done(((f32[32,4,128]{2,0,1:T(8,128)}), f32[16,4,128]{2,0,1:T(8,128)}) %reduce-scatter.9.cloned.1.call-update) | async-done | bytes 32784 | tf_op jit(solution)/shard_map/reduce_scatter | solution.py:46
  1559.4 1.3 dynamic-slice
  1560.8 12.9 reduce-scatter.11.cloned.1.call-done
  1574.4 29.7 %all-reduce = f32[8,4,128]{2,1,0:T(4,128)S(1)} all-reduce(f32[8,4,128]{2,1,0:T(4,128)S(1)} %copy.25), channel_id=6, replica_groups=mesh['tm_0'=4,'tm_1'=2,'tm_2'=2,'cell_0'=8,'cell_1'=4] {'cell_0'}, use_global_device_ids=true, to_apply=%region_4.5.clone | all-reduce | flops 4096 | bytes 32768
  1604.1 1.3 dynamic-slice_bitcast_fusion
  (31 shorter events, 4.1 us)
Async XLA Ops:
  6.5 1270.1 %copy-start = (f32[16,16]{1,0:T(8,128)S(1)}, f32[16,16]{1,0:T(8,128)}, u32[]{:S(2)}) copy-start(f32[16,16]{1,0:T(8,128)} %param.8) | copy-start | bytes 3076
  6.5 1425.1 %all-gather.3.cloned.1.call-start = ((), (), s32[]{:S(2)}) async-start(), calls=%async_computation.7 | async-start | bytes 4325376 | tf_op jit(solution)/shard_map/all_gather | solution.py:95
  1145.7 131.9 %copy-start.3 = (s32[2,512]{1,0:T(2,128)S(1)}, s32[2,512]{1,0:T(2,128)}, u32[]{:S(2)}) copy-start(s32[2,512]{1,0:T(2,128)} %param.9) | copy-start | bytes 12292
  1145.7 136.4 %copy-start.2 = (s32[2048]{0:T(1024)S(1)}, s32[2048]{0:T(1024)}, u32[]{:S(2)}) copy-start(s32[2048]{0:T(1024)} %param.11) | copy-start | bytes 24580
  1278.3 17.0 %all-to-all-start = ((s32[32,2,512]{2,1,0:T(2,128)}), s32[32,2,512]{2,1,0:T(2,128)S(1)}, u32[]{:S(2)}, u32[]{:S(2)}) async-start(s32[32,2,512]{2,1,0:T(2,128)} %broadcast_in_dim.33), calls=%async_computation | async-start | bytes 262144 | tf_op jit(solution)/shard_map/all_to_all | solution.py:21
  1431.6 30.7 %copy-start.1 = (bf16[2048,512]{1,0:T(8,128)(2,1)S(1)}, bf16[2048,512]{1,0:T(8,128)(2,1)}, u32[]{:S(2)}) copy-start(bf16[2048,512]{1,0:T(8,128)(2,1)} %gather_fusion) | copy-start | bytes 6291460
  1455.3 15.8 all-to-all-start.2
  1462.2 44.2 %reduce-scatter.5.cloned.1.call-start = ((), (), s32[]{:S(2)}) async-start(), calls=%async_computation.8 | async-start | bytes 1310720 | tf_op jit(solution)/shard_map/reduce_scatter | solution.py:46
  1473.5 59.7 %reduce-scatter.7.cloned.1.call-start = ((), (), s32[]{:S(2)}) async-start(), calls=%async_computation.9 | async-start | bytes 327680 | tf_op jit(solution)/shard_map/reduce_scatter | solution.py:46
  1506.5 52.9 %reduce-scatter.9.cloned.1.call-start = ((), (), s32[]{:S(2)}) async-start(), calls=%async_computation.10 | async-start | bytes 98304 | tf_op jit(solution)/shard_map/reduce_scatter | solution.py:46
  1533.2 40.5 %reduce-scatter.11.cloned.1.call-start = ((), (), s32[]{:S(2)}) async-start(), calls=%async_computation.11 | async-start | bytes 49152 | tf_op jit(solution)/shard_map/reduce_scatter | solution.py:46
Sparse Core Ops, SparseCore 0:
  1277.7 153.8 all-gather.2
  1473.6 32.7 reduce-scatter.4
  1509.5 23.6 reduce-scatter.6
  1535.8 23.5 reduce-scatter.8
  1562.0 11.6 reduce-scatter.10
where the time goes:
time: 1610 us
  blocking collectives  1290 us (80%)
  waiting for transfers between devices  243 us (15%)
  matrix products  25.9 us (2%)
  local copies, waits for them, and re-layouts  18.6 us (1%)
    all_gather x1, blocking collectives, per_device(): lax.all_gather(duals, TM_CELL, axis=0, tiled=True)  1140 us
    all_gather x1, waiting for transfers between devices, per_device(): portion = lax.all_gather(values, CELL, axis=0, tiled=True)  136 us
    all_to_all x1, blocking collectives, per_device(): lax.all_to_all(local_adj, TM, split_axis=2, concat_axis=1, tiled=True)  126 us
    reduce_scatter x4, waiting for transfers between devices, own_block(): pieces = lax.psum_scatter(pieces, axes[k], scatter_dimension=0, tiled=True)  98.7 us
  transfers between devices with their start and end apart: 7, of which 7 were waited for; matrix products, arithmetic and copies ran while one was open for 1% of the time, Pallas kernels for 0%

commit v1 on v0

--- a/solution.py
+++ b/solution.py
@@ -88,7 +88,9 @@
         adjoint.astype(jnp.bfloat16).reshape(time_count, cell_count, real_count).transpose(1, 0, 2)
     )
     all_coords = gathered_copies(cell_coords, CELL, 1)
-    spread_adj = lax.all_to_all(local_adj, TM, split_axis=2, concat_axis=1, tiled=True)
+    spread_adj = jnp.concatenate(
+        lax.all_to_all(jnp.stack(jnp.split(local_adj, lax.axis_size(TM), axis=2)), TM, 0, 0), axis=1
+    )
     values = jnp.einsum(
         "st,ctr->csr", time_cov, spread_adj.astype(jnp.float32), precision=lax.Precision.HIGHEST
     ).astype(jnp.bfloat16)

time: 1610 us -> 1610 us (level)
  no operation moved by 1% of the time
where the time goes in v1:
time: 1610 us
  blocking collectives  1290 us (80%)
  waiting for transfers between devices  243 us (15%)
  matrix products  25.6 us (2%)
  local copies, waits for them, and re-layouts  17.7 us (1%)
    all_gather x1, blocking collectives, per_device(): lax.all_gather(duals, TM_CELL, axis=0, tiled=True)  1140 us
    all_gather x1, waiting for transfers between devices, per_device(): portion = lax.all_gather(values, CELL, axis=0, tiled=True)  137 us
    all_to_all x1, blocking collectives, per_device(): lax.all_to_all(jnp.stack(jnp.split(local_adj, lax.axis_size(TM), axis=2))...  126 us
    reduce_scatter x4, waiting for transfers between devices, own_block(): pieces = lax.psum_scatter(pieces, axes[k], scatter_dimension=0, tiled=True)  98 us
  transfers between devices with their start and end apart: 7, of which 7 were waited for; matrix products, arithmetic and copies ran while one was open for 1% of the time, Pallas kernels for 0%

profile of v1, /device:TPU:2, one launch (start us, length us, event | category | flops | bytes accessed | tf_op | source)
XLA Modules:
  0.0 1609.0 jit_solution(10315204574507560594)
XLA Ops:
  6.5 1138.5 %all-gather = bf16[512,4,128]{2,1,0:T(4,128)(2,1)S(1)} all-gather(bf16[1,4,128]{2,1,0:T(4,128)(2,1)} %bitcast.117), channel_id=1, replica_groups=mesh['tm_0'=4,'tm_1'=2,'tm_2'=2,'cell_0'=8,'cell_1'=4] {'tm_0','tm_1','t..., dimensions={0}, use_global_device_ids=true | all-gather | bytes 525312 | tf_op jit(solution)/shard_map/all_gather | solution.py:83
  1145.7 1.8 select_bitcast_fusion
  1148.2 126.0 %all_to_all.19 = bf16[16,512,1,8]{1,3,2,0:T(8,128)(2,1)S(1)} all-to-all(bf16[16,512,1,8]{1,3,2,0:T(8,128)(2,1)S(1)} %constant_dynamic-update-slice_fusion), channel_id=1, replica_groups=mesh['tm_0'=4,'tm_1'=2,'tm_2'=2,'cell_0'=8,'cell_1'=4] {'tm_0','tm_1','t..., dimensions={0} | all-to-all | bytes 262144 | tf_op jit(solution)/shard_map/all_to_all | solution.py:92
  1274.2 0.9 fusion.15
  1275.8 3.8 all-to-all-start
  1279.7 9.2 gather_fusion
  1288.9 3.8 all-to-all-done
  1292.8 136.6 %all-gather.3.cloned.1.call-done = bf16[16384,16,8]{0,1,2:T(8,128)(2,1)} async-done(((bf16[512,16,8]{0,1,2:T(8,128)(2,1)}), bf16[16384,16,8]{0,1,2:T(8,128)(2,1)}) %all-gather.3.cloned.1.call-update) | async-done | bytes 4194320 | tf_op jit(solution)/shard_map/all_gather | solution.py:97
  1429.4 22.9 %fusion.9 = bf16[512,16,8]{0,1,2:T(8,128)(2,1)S(1)} fusion(bf16[16384,16,8]{0,1,2:T(8,128)(2,1)} %all-gather.3.cloned.1.call-done, s32[16384]{0:T(1024)S(1)} %bitcast.114, s32[512]{0:T(512)S(1)} %bitcast.116, s32[16384]{0:T(1024)S(1)} %bitcast.113, s32[512]{0:T(512)S(1)} %bitcast.115), kind=kOutput, calls=%fused_computation.12 | convolution fusion | flops 2239823872 | bytes 4460544 | tf_op jit(solution)/shard_map/dot_general | solution.py:99
  1452.3 0.7 copy.19
  1453.1 6.9 all-to-all-start.2
  1460.0 1.6 broadcast_select_fusion
  1461.6 2.5 select_n.30
  1464.2 4.6 all-to-all-done.2
  1468.8 1.3 fusion.6
  1470.1 1.1 copy.22
  1471.3 32.2 %reduce-scatter.5.cloned.1.call-done = f32[128,4,128]{2,0,1:T(8,128)} async-done(((f32[512,4,128]{2,0,1:T(8,128)}), f32[128,4,128]{2,0,1:T(8,128)}) %reduce-scatter.5.cloned.1.call-update) | async-done | bytes 262160 | tf_op jit(solution)/shard_map/reduce_scatter | solution.py:46
  1503.6 26.7 %reduce-scatter.7.cloned.1.call-done = f32[32,4,128]{2,0,1:T(8,128)} async-done(((f32[128,4,128]{2,0,1:T(8,128)}), f32[32,4,128]{2,0,1:T(8,128)}) %reduce-scatter.7.cloned.1.call-update) | async-done | bytes 65552 | tf_op jit(solution)/shard_map/reduce_scatter | solution.py:46
  1530.3 26.2 %reduce-scatter.9.cloned.1.call-done = f32[16,4,128]{2,0,1:T(8,128)} async-done(((f32[32,4,128]{2,0,1:T(8,128)}), f32[16,4,128]{2,0,1:T(8,128)}) %reduce-scatter.9.cloned.1.call-update) | async-done | bytes 32784 | tf_op jit(solution)/shard_map/reduce_scatter | solution.py:46
  1556.5 1.3 dynamic-slice
  1557.9 12.9 reduce-scatter.11.cloned.1.call-done
  1570.8 0.7 copy.23
  1571.5 29.7 %all-reduce = f32[8,4,128]{2,1,0:T(4,128)S(1)} all-reduce(f32[8,4,128]{2,1,0:T(4,128)S(1)} %copy.23), channel_id=6, replica_groups=mesh['tm_0'=4,'tm_1'=2,'tm_2'=2,'cell_0'=8,'cell_1'=4] {'cell_0'}, use_global_device_ids=true, to_apply=%region_4.5.clone | all-reduce | flops 4096 | bytes 32768
  1601.2 1.2 dynamic-slice_bitcast_fusion
  (41 shorter events, 2.3 us)
Async XLA Ops:
  6.5 1267.7 %copy-start = (f32[16,16]{1,0:T(8,128)S(1)}, f32[16,16]{1,0:T(8,128)}, u32[]{:S(2)}) copy-start(f32[16,16]{1,0:T(8,128)} %param.8) | copy-start | bytes 3076
  6.5 1422.9 %all-gather.3.cloned.1.call-start = ((), (), s32[]{:S(2)}) async-start(), calls=%async_computation.7 | async-start | bytes 4325376 | tf_op jit(solution)/shard_map/all_gather | solution.py:97
  6.5 1268.6 %copy-start.3 = (s32[2,512]{1,0:T(2,128)S(1)}, s32[2,512]{1,0:T(2,128)}, u32[]{:S(2)}) copy-start(s32[2,512]{1,0:T(2,128)} %param.9) | copy-start | bytes 12292
  1145.7 133.9 %copy-start.2 = (s32[2048]{0:T(1024)S(1)}, s32[2048]{0:T(1024)}, u32[]{:S(2)}) copy-start(s32[2048]{0:T(1024)} %param.11) | copy-start | bytes 24580
  1275.8 16.9 %all-to-all-start = ((s32[32,2,512]{2,1,0:T(2,128)}), s32[32,2,512]{2,1,0:T(2,128)S(1)}, u32[]{:S(2)}, u32[]{:S(2)}) async-start(s32[32,2,512]{2,1,0:T(2,128)} %broadcast_in_dim.33), calls=%async_computation | async-start | bytes 262144 | tf_op jit(solution)/shard_map/all_to_all | solution.py:21
  1429.4 30.6 %copy-start.1 = (bf16[2048,512]{1,0:T(8,128)(2,1)S(1)}, bf16[2048,512]{1,0:T(8,128)(2,1)}, u32[]{:S(2)}) copy-start(bf16[2048,512]{1,0:T(8,128)(2,1)} %gather_fusion) | copy-start | bytes 6291460
  1453.1 15.7 all-to-all-start.2
  1460.0 43.5 %reduce-scatter.5.cloned.1.call-start = ((), (), s32[]{:S(2)}) async-start(), calls=%async_computation.8 | async-start | bytes 1310720 | tf_op jit(solution)/shard_map/reduce_scatter | solution.py:46
  1471.2 59.0 %reduce-scatter.7.cloned.1.call-start = ((), (), s32[]{:S(2)}) async-start(), calls=%async_computation.9 | async-start | bytes 327680 | tf_op jit(solution)/shard_map/reduce_scatter | solution.py:46
  1503.5 53.0 %reduce-scatter.9.cloned.1.call-start = ((), (), s32[]{:S(2)}) async-start(), calls=%async_computation.10 | async-start | bytes 98304 | tf_op jit(solution)/shard_map/reduce_scatter | solution.py:46
  1530.3 40.5 %reduce-scatter.11.cloned.1.call-start = ((), (), s32[]{:S(2)}) async-start(), calls=%async_computation.11 | async-start | bytes 49152 | tf_op jit(solution)/shard_map/reduce_scatter | solution.py:46
Sparse Core Ops, SparseCore 0:
  1275.2 154.1 all-gather.2
  1471.4 32.1 reduce-scatter.4
  1506.6 23.6 reduce-scatter.6
  1532.8 23.6 reduce-scatter.8
  1559.1 11.6 reduce-scatter.10
